TPU v7x, 32 devices: a whole 2x2x4 slice. The times are simulated.
32 devices in a mesh: parts: 2 (over y), warp: 4 (over z), weft: 2 (over x), ply: 2 (over core).
Axes of the slice: x: 2, y: 2, z: 4, core: 2. Of those that a mesh axis runs over, the one named last changes fastest.
Arguments:
- lam_start: float32 [64, 256, 512], P(('parts', 'warp', 'ply'), 'weft'), parts along dimension 0, as said below
- resid_start: float32 [64, 256, 512], P(('parts', 'warp', 'ply'), 'weft'), parts along dimension 0, as said below
- dirn_start: float32 [64, 256, 512], P(('parts', 'warp', 'ply'), 'weft'), parts along dimension 0, as said below
- rz_start: float32 [2], P('parts'), parts along dimension 0, may hold values from 10485760 to 83886080
- pattern: int32 [64, 256], P(('parts', 'warp', 'ply'), 'weft'), parts along dimension 0, may hold values from 0 to 2
- corners: int32 [4, 64, 256], P(None, ('parts', 'warp', 'ply'), 'weft'), parts along dimension 1, may hold values from -1 to 127, as said below
- schur_inv: float32 [3, 512, 512], replicated, as said below
- schur_dirichlet: float32 [3, 512, 512], replicated, as said below
- corner_shape: float32 [3, 4, 512], replicated, may hold values from -0.3 to 0.3
- coarse_inv: float32 [256, 128], P(('parts', 'warp', 'weft', 'ply')), parts along dimension 0, as said below
Outputs:
- lam_final: float32 [64, 256, 512], P(('parts', 'warp', 'ply'), 'weft'), parts along dimension 0
- resid_final: float32 [64, 256, 512], P(('parts', 'warp', 'ply'), 'weft'), parts along dimension 0
- dirn_final: float32 [64, 256, 512], P(('parts', 'warp', 'ply'), 'weft'), parts along dimension 0
There are 2 independent parts, one for each index of `parts`. A program takes and returns all parts, laid end to end along the dimension named above; an argument that names none is the same for every part. Nothing has to cross between parts.
Inputs may be any that keep to these rules, and one draw needn't show every extreme that they name: `lam_start`: in each cell the W block is minus the E block of the cell to its west and zero where j = 0; the S block is minus the N block of the cell to its south and zero where i = 0. `resid_start`: in each cell the W block is minus the E block of the cell to its west and zero where j = 0; the S block is minus the N block of the cell to its south and zero where i = 0. `dirn_start`: in each cell the W block is minus the E block of the cell to its west and zero where j = 0; the S block is minus the N block of the cell to its south and zero where i = 0. `corners`: corner k of cell (i, j) is the corner node (i, j), (i, j + 1), (i + 1, j) or (i + 1, j + 1) for k = 0, 1, 2, 3; nodes (a, b) with a = 32 or b = 256 are -1; every other node's row is that of its aggregate, the block of 8 x 8 nodes with the same a // 8 and b // 8; each aggregate has its own row, and which aggregate has which row is drawn. `schur_inv`: each matrix is symmetric positive definite. `schur_dirichlet`: each matrix is symmetric positive definite. `coarse_inv`: symmetric positive definite.
All inputs are finite; a program needn't handle non-finite values.
Results may differ from a plain program's by a relative error of at most 0.00027.
Values sent between devices are 32-bit elements; how exact they have to be, the bound alone decides.
A program may use at most 64 MiB of HBM per device.

v0:
```python
import jax
import jax.numpy as jnp
from jax import lax
from jax.sharding import PartitionSpec as P

ITERS = 3
HIGHEST = lax.Precision.HIGHEST


def with_halo(array, sides, width):
    for axis, dim in sides:
        count, length = (lax.axis_size(axis), array.shape[dim])
        up = [(i, (i + 1) % count) for i in range(count - 1)]
        down = [(j, i) for i, j in up]
        last = lax.slice_in_dim(array, length - width, length, axis=dim)
        leading = lax.slice_in_dim(array, 0, width, axis=dim)
        before = lax.ppermute(last, axis, up)
        after = lax.ppermute(leading, axis, down)
        array = jnp.concatenate([before, array, after], axis=dim)
    return array


def split_edges(values, edge_len):
    return (
        values[..., :edge_len],
        values[..., edge_len : 2 * edge_len],
        values[..., 2 * edge_len : 3 * edge_len],
        values[..., 3 * edge_len :],
    )


def cross_faces(values, edge_len, west_keep, south_keep):
    west_side, east_side, south_side, north_side = split_edges(values, edge_len)
    rows_here, cols_here = (values.shape[0], values.shape[1])
    local_row = lax.broadcasted_iota(jnp.int32, (rows_here, cols_here, 1), 0)
    local_col = lax.broadcasted_iota(jnp.int32, (rows_here, cols_here, 1), 1)
    along_rows = jnp.where(local_row == 0, south_side, north_side)
    along_cols = jnp.where(local_col == 0, west_side, east_side)
    padded = with_halo(
        jnp.concatenate([along_rows, along_cols], axis=2), ((("warp", "ply"), 0), ("weft", 1)), 1
    )
    from_south = padded[0, 1:-1, :edge_len]
    from_north = padded[-1, 1:-1, :edge_len]
    from_west = padded[1:-1, 0, edge_len:]
    from_east = padded[1:-1, -1, edge_len:]
    east_west = jnp.concatenate([west_side[:, 1:], from_east[:, None]], axis=1)
    west_east = jnp.concatenate([from_west[:, None], east_side[:, :-1]], axis=1)
    north_south = jnp.concatenate([south_side[1:], from_north[None]], axis=0)
    south_north = jnp.concatenate([from_south[None], north_side[:-1]], axis=0)
    return jnp.concatenate(
        [
            (west_side - west_east) * west_keep,
            east_side - east_west,
            (south_side - south_north) * south_keep,
            north_side - north_south,
        ],
        axis=2,
    )


def apply_cells(rows_flat, matrices, cell_order, inverse, group_sizes):
    sorted_rows = rows_flat[cell_order]
    product = lax.ragged_dot(
        sorted_rows, matrices, group_sizes, precision=HIGHEST, preferred_element_type=jnp.float32
    )
    return product[inverse]


def on_device(
    lam_start,
    resid_start,
    dirn_start,
    rz_start,
    pattern,
    corners,
    schur_inv,
    schur_dirichlet,
    corner_shape,
    coarse_inv,
):
    rows_here, cols_here, dof_count = lam_start.shape
    edge_len = dof_count // 4
    pattern_count = schur_inv.shape[0]
    coarse_count = coarse_inv.shape[1]
    row_pos = (
        lax.broadcasted_iota(jnp.int32, (rows_here, cols_here, 1), 0)
        + lax.axis_index(("warp", "ply")) * rows_here
    )
    col_pos = (
        lax.broadcasted_iota(jnp.int32, (rows_here, cols_here, 1), 1)
        + lax.axis_index("weft") * cols_here
    )
    total_rows = lax.axis_size(("warp", "ply")) * rows_here
    total_cols = lax.axis_size("weft") * cols_here
    west_keep = (col_pos > 0).astype(jnp.float32)
    south_keep = (row_pos > 0).astype(jnp.float32)
    east_weight = jnp.where(col_pos == total_cols - 1, 1.0, 0.5).astype(jnp.float32)
    north_weight = jnp.where(row_pos == total_rows - 1, 1.0, 0.5).astype(jnp.float32)
    block_shape = (rows_here, cols_here, edge_len)
    edge_weight = jnp.concatenate(
        [
            jnp.broadcast_to(0.5 * west_keep, block_shape),
            jnp.broadcast_to(east_weight, block_shape),
            jnp.broadcast_to(0.5 * south_keep, block_shape),
            jnp.broadcast_to(north_weight, block_shape),
        ],
        axis=2,
    )
    cell_kind = pattern.reshape(-1)
    cell_order = jnp.argsort(cell_kind, stable=True)
    inverse = jnp.argsort(cell_order, stable=True)
    selector = (cell_kind[None, :] == jnp.arange(pattern_count, dtype=jnp.int32)[:, None]).astype(
        jnp.float32
    )
    group_sizes = jnp.sum(selector, axis=1).astype(jnp.int32)
    corner_rows = corners.reshape(4, -1)
    corner_live = corner_rows >= 0
    corner_slot = jnp.where(corner_live, corner_rows, coarse_count)
    corner_pick = jnp.where(corner_live, corner_rows, 0)
    multiplier, residual, direction = (lam_start, resid_start, dirn_start)
    rz_prev = rz_start[0]
    for iteration in range(ITERS):
        scaled = (edge_weight * residual).reshape(-1, dof_count)
        spread = apply_cells(scaled, schur_dirichlet, cell_order, inverse, group_sizes).reshape(
            residual.shape
        )
        precond = edge_weight * cross_faces(spread, edge_len, west_keep, south_keep)
        rz_now = lax.psum(jnp.sum(edge_weight * residual * precond), ("warp", "weft", "ply"))
        direction = precond + rz_now / rz_prev * direction
        rows_flat = direction.reshape(-1, dof_count)
        local_image = apply_cells(rows_flat, schur_inv, cell_order, inverse, group_sizes)
        corner_terms = jnp.einsum("pkd,cd->pkc", corner_shape, rows_flat, precision=HIGHEST)
        corner_load = jnp.sum(corner_terms * selector[:, None, :], axis=0)
        partial_rhs = jax.ops.segment_sum(
            corner_load.reshape(-1), corner_slot.reshape(-1), num_segments=coarse_count + 1
        )[:coarse_count]
        coarse_rhs = lax.psum(partial_rhs, ("warp", "weft", "ply"))
        coarse_sol = lax.all_gather(
            jnp.dot(coarse_inv, coarse_rhs, precision=HIGHEST),
            ("warp", "weft", "ply"),
            axis=0,
            tiled=True,
        )
        corner_vals = jnp.where(corner_live, coarse_sol[corner_pick], 0.0)
        full_image = local_image + jnp.einsum(
            "pkc,pkd->cd", selector[:, None, :] * corner_vals[None], corner_shape, precision=HIGHEST
        )
        applied = cross_faces(full_image.reshape(direction.shape), edge_len, west_keep, south_keep)
        curvature = lax.psum(jnp.sum(edge_weight * direction * applied), ("warp", "weft", "ply"))
        alpha_step = rz_now / curvature
        multiplier = multiplier + alpha_step * direction
        residual = residual - alpha_step * applied
        rz_prev = rz_now
    return (multiplier, residual, direction)


def solution(mesh):
    return jax.shard_map(
        on_device,
        mesh=mesh,
        in_specs=(
            P(("parts", "warp", "ply"), "weft", None),
            P(("parts", "warp", "ply"), "weft", None),
            P(("parts", "warp", "ply"), "weft", None),
            P("parts"),
            P(("parts", "warp", "ply"), "weft"),
            P(None, ("parts", "warp", "ply"), "weft"),
            P(),
            P(),
            P(),
            P(("parts", "warp", "weft", "ply"), None),
        ),
        out_specs=(
            P(("parts", "warp", "ply"), "weft", None),
            P(("parts", "warp", "ply"), "weft", None),
            P(("parts", "warp", "ply"), "weft", None),
        ),
        check_vma=False,
    )
```

profile of v0, /device:TPU:0, one launch (start us, length us, event | category | flops | bytes accessed | tf_op | source)
XLA Modules:
  0.0 678.7 jit_solution(7160559662432840204)
XLA Ops:
  15.8 8.7 %ragged-dot-none.5 = f32[512,512]{1,0:T(8,128)} custom-call(s32[1]{0:T(128)} %get-tuple-element.27, s32[4]{0:T(128)} %get-tuple-element.28, s32[4]{0:T(128)} %get-tuple-element.29, s32[4]{0:T(128)} %get-tuple-element.30, s32[1]{0:T(128)} %get-tuple-element.27, f32[512,512]{1,0:T(8,128)} %gather_fusion, f32[3,512,512]{2,1,0:T(8,128)} %param.17), custom_call_target="tpu_custom_call" | custom-call | flops 268435456 | bytes 5242892 | tf_op jit(solution)/shard_map/ragged_dot_general/ragged-dot-none
  50.5 33.6 %psum.63 = f32[]{:T(128)} all-reduce(f32[]{:T(128)} %multiply_reduce_fusion.2), channel_id=1, replica_groups=mesh['parts'=2,'warp'=4,'weft'=2,'ply'=2] {'warp','weft','ply'}, use_global_device_ids=true, to_apply=%region_4.5 | all-reduce | flops 1 | bytes 8 | tf_op jit(solution)/shard_map/psum | solution.py:128
  87.2 14.7 %scatter_custom_fusion = f32[129]{0:T(256)S(1)} fusion(s32[2048]{0:T(1024)S(1)} %bitcast.138, f32[2048]{0:T(1024)S(1)} %bitcast.142, f32[]{:T(128)} %constant.17.clone.1), kind=kCustom, calls=%fused_computation.187 | custom fusion | flops 2048 | bytes 520 | tf_op jit(solution)/shard_map/scatter-add | solution.py:134
  101.8 29.5 %psum.64 = f32[128]{0:T(128)S(1)} all-reduce(f32[128]{0:T(128)S(1)} %slice.337), channel_id=1, replica_groups=mesh['parts'=2,'warp'=4,'weft'=2,'ply'=2] {'warp','weft','ply'}, use_global_device_ids=true, to_apply=%region_7.8 | all-reduce | flops 128 | bytes 1024 | tf_op jit(solution)/shard_map/psum | solution.py:137
  131.7 29.5 %all-reduce = f32[128]{0:T(128)S(1)} all-reduce(f32[128]{0:T(128)S(1)} %dynamic-update-slice), channel_id=1, replica_groups=mesh['parts'=2,'warp'=4,'weft'=2,'ply'=2] {'warp','weft','ply'}, use_global_device_ids=true, to_apply=%add | all-reduce | flops 128 | bytes 1024
  161.1 12.6 %gather_fusion.4 = f32[2048]{0:T(1024)S(1)} fusion(f32[128]{0:T(128)S(1)} %all-reduce, s32[2048]{0:T(1024)S(1)} %broadcast_clamp_fusion), kind=kCustom, calls=%fused_computation.4 | custom fusion | bytes 24576 | tf_op jit(solution)/shard_map/gather | solution.py:144
  176.1 8.7 %ragged-dot-none.4 = f32[512,512]{1,0:T(8,128)} custom-call(s32[1]{0:T(128)} %get-tuple-element.27, s32[4]{0:T(128)} %get-tuple-element.28, s32[4]{0:T(128)} %get-tuple-element.29, s32[4]{0:T(128)} %get-tuple-element.30, s32[1]{0:T(128)} %get-tuple-element.27, f32[512,512]{1,0:T(8,128)} %gather_fusion.2, f32[3,512,512]{2,1,0:T(8,128)} %param.16), custom_call_target="tpu_custom_call" | custom-call | flops 268435456 | bytes 5242892 | tf_op jit(solution)/shard_map/ragged_dot_general/ragged-dot-none
  205.1 32.0 %psum.65 = f32[]{:T(128)} all-reduce(f32[]{:T(128)} %fusion.23), channel_id=1, replica_groups=mesh['parts'=2,'warp'=4,'weft'=2,'ply'=2] {'warp','weft','ply'}, use_global_device_ids=true, to_apply=%region_9.10 | all-reduce | flops 1 | bytes 8 | tf_op jit(solution)/shard_map/psum | solution.py:149
  242.4 8.7 %ragged-dot-none.3 = f32[512,512]{1,0:T(8,128)} custom-call(s32[1]{0:T(128)} %get-tuple-element.27, s32[4]{0:T(128)} %get-tuple-element.28, s32[4]{0:T(128)} %get-tuple-element.29, s32[4]{0:T(128)} %get-tuple-element.30, s32[1]{0:T(128)} %get-tuple-element.27, f32[512,512]{1,0:T(8,128)} %gather_fusion.5, f32[3,512,512]{2,1,0:T(8,128)} %param.17), custom_call_target="tpu_custom_call" | custom-call | flops 268435456 | bytes 5242892 | tf_op jit(solution)/shard_map/ragged_dot_general/ragged-dot-none
  270.0 30.6 %psum.66 = f32[]{:T(128)} all-reduce(f32[]{:T(128)} %multiply_reduce_fusion.1), channel_id=1, replica_groups=mesh['parts'=2,'warp'=4,'weft'=2,'ply'=2] {'warp','weft','ply'}, use_global_device_ids=true, to_apply=%region_11.12 | all-reduce | flops 1 | bytes 8 | tf_op jit(solution)/shard_map/psum | solution.py:128
  304.3 14.7 %scatter_custom_fusion.1 = f32[129]{0:T(256)S(1)} fusion(s32[2048]{0:T(1024)S(1)} %bitcast.139, f32[2048]{0:T(1024)S(1)} %bitcast.143, f32[]{:T(128)} %constant.17.clone.1), kind=kCustom, calls=%fused_computation.185 | custom fusion | flops 2048 | bytes 520 | tf_op jit(solution)/shard_map/scatter-add | solution.py:134
  319.0 29.5 %psum.67 = f32[128]{0:T(128)S(1)} all-reduce(f32[128]{0:T(128)S(1)} %slice.370), channel_id=1, replica_groups=mesh['parts'=2,'warp'=4,'weft'=2,'ply'=2] {'warp','weft','ply'}, use_global_device_ids=true, to_apply=%region_14.15 | all-reduce | flops 128 | bytes 1024 | tf_op jit(solution)/shard_map/psum | solution.py:137
  348.8 29.5 %all-reduce.1 = f32[128]{0:T(128)S(1)} all-reduce(f32[128]{0:T(128)S(1)} %dynamic-update-slice.1), channel_id=1, replica_groups=mesh['parts'=2,'warp'=4,'weft'=2,'ply'=2] {'warp','weft','ply'}, use_global_device_ids=true, to_apply=%add.1 | all-reduce | flops 128 | bytes 1024
  378.3 12.6 %gather_fusion.9 = f32[2048]{0:T(1024)S(1)} fusion(f32[128]{0:T(128)S(1)} %all-reduce.1, s32[2048]{0:T(1024)S(1)} %broadcast_clamp_fusion), kind=kCustom, calls=%fused_computation.9 | custom fusion | bytes 24576 | tf_op jit(solution)/shard_map/gather | solution.py:144
  393.3 8.7 %ragged-dot-none.2 = f32[512,512]{1,0:T(8,128)} custom-call(s32[1]{0:T(128)} %get-tuple-element.27, s32[4]{0:T(128)} %get-tuple-element.28, s32[4]{0:T(128)} %get-tuple-element.29, s32[4]{0:T(128)} %get-tuple-element.30, s32[1]{0:T(128)} %get-tuple-element.27, f32[512,512]{1,0:T(8,128)} %gather_fusion.7, f32[3,512,512]{2,1,0:T(8,128)} %param.16), custom_call_target="tpu_custom_call" | custom-call | flops 268435456 | bytes 5242892 | tf_op jit(solution)/shard_map/ragged_dot_general/ragged-dot-none
  422.3 32.2 %psum.68 = f32[]{:T(128)} all-reduce(f32[]{:T(128)} %fusion.22), channel_id=1, replica_groups=mesh['parts'=2,'warp'=4,'weft'=2,'ply'=2] {'warp','weft','ply'}, use_global_device_ids=true, to_apply=%region_16.17 | all-reduce | flops 1 | bytes 8 | tf_op jit(solution)/shard_map/psum | solution.py:149
  461.6 8.7 %ragged-dot-none.1 = f32[512,512]{1,0:T(8,128)} custom-call(s32[1]{0:T(128)} %get-tuple-element.27, s32[4]{0:T(128)} %get-tuple-element.28, s32[4]{0:T(128)} %get-tuple-element.29, s32[4]{0:T(128)} %get-tuple-element.30, s32[1]{0:T(128)} %get-tuple-element.27, f32[512,512]{1,0:T(8,128)} %gather_fusion.10, f32[3,512,512]{2,1,0:T(8,128)} %param.17), custom_call_target="tpu_custom_call" | custom-call | flops 268435456 | bytes 5242892 | tf_op jit(solution)/shard_map/ragged_dot_general/ragged-dot-none
  488.3 30.6 %psum.69 = f32[]{:T(128)} all-reduce(f32[]{:T(128)} %multiply_reduce_fusion), channel_id=1, replica_groups=mesh['parts'=2,'warp'=4,'weft'=2,'ply'=2] {'warp','weft','ply'}, use_global_device_ids=true, to_apply=%region_18.19 | all-reduce | flops 1 | bytes 8 | tf_op jit(solution)/shard_map/psum | solution.py:128
  522.9 14.7 %scatter_custom_fusion.2 = f32[129]{0:T(256)S(1)} fusion(s32[2048]{0:T(1024)S(1)} %bitcast.140, f32[2048]{0:T(1024)S(1)} %bitcast.141, f32[]{:T(128)} %constant.17.clone.1), kind=kCustom, calls=%fused_computation.183 | custom fusion | flops 2048 | bytes 520 | tf_op jit(solution)/shard_map/scatter-add | solution.py:134
  537.5 29.5 %psum.70 = f32[128]{0:T(128)S(1)} all-reduce(f32[128]{0:T(128)S(1)} %slice.403), channel_id=1, replica_groups=mesh['parts'=2,'warp'=4,'weft'=2,'ply'=2] {'warp','weft','ply'}, use_global_device_ids=true, to_apply=%region_21.22 | all-reduce | flops 128 | bytes 1024 | tf_op jit(solution)/shard_map/psum | solution.py:137
  567.4 29.5 %all-reduce.2 = f32[128]{0:T(128)S(1)} all-reduce(f32[128]{0:T(128)S(1)} %dynamic-update-slice.2), channel_id=1, replica_groups=mesh['parts'=2,'warp'=4,'weft'=2,'ply'=2] {'warp','weft','ply'}, use_global_device_ids=true, to_apply=%add.2 | all-reduce | flops 128 | bytes 1024
  596.8 12.6 %gather_fusion.14 = f32[2048]{0:T(1024)S(1)} fusion(f32[128]{0:T(128)S(1)} %all-reduce.2, s32[2048]{0:T(1024)S(1)} %broadcast_clamp_fusion), kind=kCustom, calls=%fused_computation.14 | custom fusion | bytes 24576 | tf_op jit(solution)/shard_map/gather | solution.py:144
  611.8 8.8 %ragged-dot-none = f32[512,512]{1,0:T(8,128)} custom-call(s32[1]{0:T(128)} %get-tuple-element.27, s32[4]{0:T(128)} %get-tuple-element.28, s32[4]{0:T(128)} %get-tuple-element.29, s32[4]{0:T(128)} %get-tuple-element.30, s32[1]{0:T(128)} %get-tuple-element.27, f32[512,512]{1,0:T(8,128)} %gather_fusion.12, f32[3,512,512]{2,1,0:T(8,128)} %param.16), custom_call_target="tpu_custom_call" | custom-call | flops 268435456 | bytes 5242892 | tf_op jit(solution)/shard_map/ragged_dot_general/ragged-dot-none
  641.1 32.1 %psum.71 = f32[]{:T(128)} all-reduce(f32[]{:T(128)} %fusion.21), channel_id=1, replica_groups=mesh['parts'=2,'warp'=4,'weft'=2,'ply'=2] {'warp','weft','ply'}, use_global_device_ids=true, to_apply=%region_23.24 | all-reduce | flops 1 | bytes 8 | tf_op jit(solution)/shard_map/psum | solution.py:149
  (280 shorter events, 166.1 us)
Async XLA Ops:
  29.4 6.2 collective-permute-start
  32.6 5.1 collective-permute-start.1
  38.5 7.7 %collective-permute-start.2 = (f32[6,1,256]{2,1,0:T(1,128)S(1)}, f32[6,1,256]{2,1,0:T(1,128)S(1)}, u32[]{:S(2)}, u32[]{:S(2)}) collective-permute-start(f32[6,1,256]{2,1,0:T(1,128)S(1)} %get-tuple-element.103), channel_id=1, source_target_pairs={{0,2},{1,3},{4,6},{5,7},{8,10},{9,11},{12,14},{13,15},{16,18},{17,... | collective-permute-start | bytes 18440 | tf_op jit(solution)/shard_map/ppermute | solution.py:17
  41.9 5.5 collective-permute-start.3
  191.2 3.1 collective-permute-start.4
  193.0 3.2 collective-permute-start.5
  196.3 2.8 collective-permute-start.6
  197.6 5.5 collective-permute-start.7
  256.5 3.7 collective-permute-start.8
  257.8 3.2 collective-permute-start.9
  261.1 2.7 collective-permute-start.10
  262.4 5.5 collective-permute-start.11
  408.4 3.1 collective-permute-start.12
  410.2 3.2 collective-permute-start.13
  413.5 2.7 collective-permute-start.14
  414.8 5.5 collective-permute-start.15
  474.6 3.9 collective-permute-start.16
  476.2 3.2 collective-permute-start.17
  479.4 3.7 collective-permute-start.18
  480.7 5.5 collective-permute-start.19
  627.0 3.3 collective-permute-start.20
  628.9 3.2 collective-permute-start.21
  632.1 2.7 collective-permute-start.22
  633.4 5.5 collective-permute-start.23
  (45 other events, 1870.4 us)
where the time goes:
time: 681 us; the launch traced here: 679 us
  blocking collectives  368 us (54%)
  local copies, waits for them, and re-layouts  88.5 us (13%)
  other arithmetic  80.7 us (12%)
  Pallas kernels  53.8 us (8%)
  starting transfers between devices  37 us (5%)
  waiting for transfers between devices  30.1 us (4%)
  matrix products  10.3 us (2%)
  between operations  10.3 us (2%)
    psum x3, blocking collectives, on_device(): lax.psum(jnp.sum(edge_weight * direction * applied), ('warp', 'weft', 'pl...  96.3 us
    psum x3, blocking collectives, on_device(): lax.psum(jnp.sum(edge_weight * residual * precond), ('warp', 'weft', 'ply'))  94.8 us
    psum x3, blocking collectives, on_device(): coarse_rhs = lax.psum(partial_rhs, ('warp', 'weft', 'ply'))  88.5 us
    unnamed x3, blocking collectives  88.4 us
    another operation x6, Pallas kernels  52.5 us
    scatter-add x3, other arithmetic, on_device(): jax.ops.segment_sum(corner_load.reshape(-1), corner_slot.reshape(-1), num...  44 us
    gather x6, local copies, waits for them, and re-layouts, on_device(): corner_vals = jnp.where(corner_live, coarse_sol[corner_pick], 0.0)  37.9 us
    ppermute x12, waiting for transfers between devices, with_halo(): after = lax.ppermute(leading, axis, down)  30.1 us
  transfers between devices with their start and end apart: 24, of which 12 were waited for; matrix products, arithmetic and copies ran while one was open for 1% of the time, Pallas kernels for 0%

commit v1 on v0

--- a/solution.py
+++ b/solution.py
@@ -134,7 +134,7 @@
         partial_rhs = jax.ops.segment_sum(
             corner_load.reshape(-1), corner_slot.reshape(-1), num_segments=coarse_count + 1
         )[:coarse_count]
-        coarse_rhs = lax.psum(partial_rhs, ("warp", "weft", "ply"))
+        coarse_rhs = jnp.sum(lax.all_gather(partial_rhs, ("warp", "weft", "ply")), axis=0)
         coarse_sol = lax.all_gather(
             jnp.dot(coarse_inv, coarse_rhs, precision=HIGHEST),
             ("warp", "weft", "ply"),

time: 681 us -> 647 us (0.950)
  blocking collectives: 368 us -> 335 us
    psum x3 -> x0, blocking collectives: 88.5 us -> none  [on_device(): coarse_rhs = lax.psum(partial_rhs, ('warp', 'weft', 'ply'))]
    all_gather x0 -> x3, blocking collectives: none -> 51.1 us  [on_device(): lax.all_gather(partial_rhs, ('warp', 'weft', 'ply'))]
where the time goes in v1:
time: 647 us; the launch traced here: 644 us
  blocking collectives  335 us (52%)
  local copies, waits for them, and re-layouts  88.5 us (14%)
  other arithmetic  80.8 us (12%)
  Pallas kernels  53.8 us (8%)
  starting transfers between devices  35.5 us (5%)
  waiting for transfers between devices  30.1 us (5%)
  matrix products  10.3 us (2%)
  between operations  10.3 us (2%)
    psum x3, blocking collectives, on_device(): lax.psum(jnp.sum(edge_weight * residual * precond), ('warp', 'weft', 'ply'))  97.6 us
    unnamed x3, blocking collectives  94.1 us
    psum x3, blocking collectives, on_device(): lax.psum(jnp.sum(edge_weight * direction * applied), ('warp', 'weft', 'pl...  92.1 us
    another operation x6, Pallas kernels  52.5 us
    all_gather x3, blocking collectives, on_device(): lax.all_gather(partial_rhs, ('warp', 'weft', 'ply'))  51.1 us
    scatter-add x3, other arithmetic, on_device(): jax.ops.segment_sum(corner_load.reshape(-1), corner_slot.reshape(-1), num...  44 us
    gather x6, local copies, waits for them, and re-layouts, on_device(): corner_vals = jnp.where(corner_live, coarse_sol[corner_pick], 0.0)  37.9 us
    ppermute x12, waiting for transfers between devices, with_halo(): after = lax.ppermute(leading, axis, down)  30.1 us
  transfers between devices with their start and end apart: 24, of which 12 were waited for; matrix products, arithmetic and copies ran while one was open for 1% of the time, Pallas kernels for 0%

profile of v1, /device:TPU:0, one launch (start us, length us, event | category | flops | bytes accessed | tf_op | source)
XLA Modules:
  0.0 644.2 jit_solution(14796568475228576509)
XLA Ops:
  15.8 8.7 %ragged-dot-none.5 = f32[512,512]{1,0:T(8,128)} custom-call(s32[1]{0:T(128)} %get-tuple-element.27, s32[4]{0:T(128)} %get-tuple-element.28, s32[4]{0:T(128)} %get-tuple-element.29, s32[4]{0:T(128)} %get-tuple-element.30, s32[1]{0:T(128)} %get-tuple-element.27, f32[512,512]{1,0:T(8,128)} %gather_fusion, f32[3,512,512]{2,1,0:T(8,128)} %param.17), custom_call_target="tpu_custom_call" | custom-call | flops 268435456 | bytes 5242892 | tf_op jit(solution)/shard_map/ragged_dot_general/ragged-dot-none
  50.5 33.6 %psum.42 = f32[]{:T(128)} all-reduce(f32[]{:T(128)} %multiply_reduce_fusion.2), channel_id=1, replica_groups=mesh['parts'=2,'warp'=4,'weft'=2,'ply'=2] {'warp','weft','ply'}, use_global_device_ids=true, to_apply=%region_4.5 | all-reduce | flops 1 | bytes 8 | tf_op jit(solution)/shard_map/psum | solution.py:128
  87.2 14.7 %scatter_custom_fusion = f32[129]{0:T(256)S(1)} fusion(s32[2048]{0:T(1024)S(1)} %bitcast.144, f32[2048]{0:T(1024)S(1)} %bitcast.148, f32[]{:T(128)} %constant.17.clone.1), kind=kCustom, calls=%fused_computation.190 | custom fusion | flops 2048 | bytes 520 | tf_op jit(solution)/shard_map/scatter-add | solution.py:134
  101.8 17.0 %all-gather.3 = f32[16,1,128]{2,1,0:T(1,128)S(1)} all-gather(f32[1,1,128]{2,1,0:T(1,128)S(1)} %slice_bitcast_fusion.2), channel_id=2, replica_groups=mesh['parts'=2,'warp'=4,'weft'=2,'ply'=2] {'warp','weft','ply'}, dimensions={0}, use_global_device_ids=true | all-gather | bytes 8704 | tf_op jit(solution)/shard_map/all_gather | solution.py:137
  119.2 31.4 %all-reduce = f32[128]{0:T(128)S(1)} all-reduce(f32[128]{0:T(128)S(1)} %dynamic-update-slice), channel_id=1, replica_groups=mesh['parts'=2,'warp'=4,'weft'=2,'ply'=2] {'warp','weft','ply'}, use_global_device_ids=true, to_apply=%add | all-reduce | flops 128 | bytes 1024
  150.6 12.6 %gather_fusion.4 = f32[2048]{0:T(1024)S(1)} fusion(f32[128]{0:T(128)S(1)} %all-reduce, s32[2048]{0:T(1024)S(1)} %broadcast_clamp_fusion), kind=kCustom, calls=%fused_computation.4 | custom fusion | bytes 24576 | tf_op jit(solution)/shard_map/gather | solution.py:144
  165.5 8.7 %ragged-dot-none.4 = f32[512,512]{1,0:T(8,128)} custom-call(s32[1]{0:T(128)} %get-tuple-element.27, s32[4]{0:T(128)} %get-tuple-element.28, s32[4]{0:T(128)} %get-tuple-element.29, s32[4]{0:T(128)} %get-tuple-element.30, s32[1]{0:T(128)} %get-tuple-element.27, f32[512,512]{1,0:T(8,128)} %gather_fusion.2, f32[3,512,512]{2,1,0:T(8,128)} %param.16), custom_call_target="tpu_custom_call" | custom-call | flops 268435456 | bytes 5242892 | tf_op jit(solution)/shard_map/ragged_dot_general/ragged-dot-none
  194.1 30.6 %psum.43 = f32[]{:T(128)} all-reduce(f32[]{:T(128)} %fusion.23), channel_id=1, replica_groups=mesh['parts'=2,'warp'=4,'weft'=2,'ply'=2] {'warp','weft','ply'}, use_global_device_ids=true, to_apply=%region_9.10 | all-reduce | flops 1 | bytes 8 | tf_op jit(solution)/shard_map/psum | solution.py:149
  230.0 8.7 %ragged-dot-none.3 = f32[512,512]{1,0:T(8,128)} custom-call(s32[1]{0:T(128)} %get-tuple-element.27, s32[4]{0:T(128)} %get-tuple-element.28, s32[4]{0:T(128)} %get-tuple-element.29, s32[4]{0:T(128)} %get-tuple-element.30, s32[1]{0:T(128)} %get-tuple-element.27, f32[512,512]{1,0:T(8,128)} %gather_fusion.5, f32[3,512,512]{2,1,0:T(8,128)} %param.17), custom_call_target="tpu_custom_call" | custom-call | flops 268435456 | bytes 5242892 | tf_op jit(solution)/shard_map/ragged_dot_general/ragged-dot-none
  257.6 32.0 %psum.44 = f32[]{:T(128)} all-reduce(f32[]{:T(128)} %multiply_reduce_fusion.1), channel_id=1, replica_groups=mesh['parts'=2,'warp'=4,'weft'=2,'ply'=2] {'warp','weft','ply'}, use_global_device_ids=true, to_apply=%region_11.12 | all-reduce | flops 1 | bytes 8 | tf_op jit(solution)/shard_map/psum | solution.py:128
  293.3 14.7 %scatter_custom_fusion.1 = f32[129]{0:T(256)S(1)} fusion(s32[2048]{0:T(1024)S(1)} %bitcast.145, f32[2048]{0:T(1024)S(1)} %bitcast.149, f32[]{:T(128)} %constant.17.clone.1), kind=kCustom, calls=%fused_computation.188 | custom fusion | flops 2048 | bytes 520 | tf_op jit(solution)/shard_map/scatter-add | solution.py:134
  308.0 17.0 %all-gather.4 = f32[16,1,128]{2,1,0:T(1,128)S(1)} all-gather(f32[1,1,128]{2,1,0:T(1,128)S(1)} %slice_bitcast_fusion.1), channel_id=3, replica_groups=mesh['parts'=2,'warp'=4,'weft'=2,'ply'=2] {'warp','weft','ply'}, dimensions={0}, use_global_device_ids=true | all-gather | bytes 8704 | tf_op jit(solution)/shard_map/all_gather | solution.py:137
  325.4 31.4 %all-reduce.1 = f32[128]{0:T(128)S(1)} all-reduce(f32[128]{0:T(128)S(1)} %dynamic-update-slice.1), channel_id=1, replica_groups=mesh['parts'=2,'warp'=4,'weft'=2,'ply'=2] {'warp','weft','ply'}, use_global_device_ids=true, to_apply=%add.1 | all-reduce | flops 128 | bytes 1024
  356.7 12.6 %gather_fusion.9 = f32[2048]{0:T(1024)S(1)} fusion(f32[128]{0:T(128)S(1)} %all-reduce.1, s32[2048]{0:T(1024)S(1)} %broadcast_clamp_fusion), kind=kCustom, calls=%fused_computation.9 | custom fusion | bytes 24576 | tf_op jit(solution)/shard_map/gather | solution.py:144
  371.7 8.7 %ragged-dot-none.2 = f32[512,512]{1,0:T(8,128)} custom-call(s32[1]{0:T(128)} %get-tuple-element.27, s32[4]{0:T(128)} %get-tuple-element.28, s32[4]{0:T(128)} %get-tuple-element.29, s32[4]{0:T(128)} %get-tuple-element.30, s32[1]{0:T(128)} %get-tuple-element.27, f32[512,512]{1,0:T(8,128)} %gather_fusion.7, f32[3,512,512]{2,1,0:T(8,128)} %param.16), custom_call_target="tpu_custom_call" | custom-call | flops 268435456 | bytes 5242892 | tf_op jit(solution)/shard_map/ragged_dot_general/ragged-dot-none
  400.2 30.8 %psum.45 = f32[]{:T(128)} all-reduce(f32[]{:T(128)} %fusion.22), channel_id=1, replica_groups=mesh['parts'=2,'warp'=4,'weft'=2,'ply'=2] {'warp','weft','ply'}, use_global_device_ids=true, to_apply=%region_16.17 | all-reduce | flops 1 | bytes 8 | tf_op jit(solution)/shard_map/psum | solution.py:149
  438.1 8.7 %ragged-dot-none.1 = f32[512,512]{1,0:T(8,128)} custom-call(s32[1]{0:T(128)} %get-tuple-element.27, s32[4]{0:T(128)} %get-tuple-element.28, s32[4]{0:T(128)} %get-tuple-element.29, s32[4]{0:T(128)} %get-tuple-element.30, s32[1]{0:T(128)} %get-tuple-element.27, f32[512,512]{1,0:T(8,128)} %gather_fusion.10, f32[3,512,512]{2,1,0:T(8,128)} %param.17), custom_call_target="tpu_custom_call" | custom-call | flops 268435456 | bytes 5242892 | tf_op jit(solution)/shard_map/ragged_dot_general/ragged-dot-none
  464.8 32.0 %psum.46 = f32[]{:T(128)} all-reduce(f32[]{:T(128)} %multiply_reduce_fusion), channel_id=1, replica_groups=mesh['parts'=2,'warp'=4,'weft'=2,'ply'=2] {'warp','weft','ply'}, use_global_device_ids=true, to_apply=%region_18.19 | all-reduce | flops 1 | bytes 8 | tf_op jit(solution)/shard_map/psum | solution.py:128
  500.8 14.7 %scatter_custom_fusion.2 = f32[129]{0:T(256)S(1)} fusion(s32[2048]{0:T(1024)S(1)} %bitcast.146, f32[2048]{0:T(1024)S(1)} %bitcast.147, f32[]{:T(128)} %constant.17.clone.1), kind=kCustom, calls=%fused_computation.186 | custom fusion | flops 2048 | bytes 520 | tf_op jit(solution)/shard_map/scatter-add | solution.py:134
  515.5 17.0 %all-gather.5 = f32[16,1,128]{2,1,0:T(1,128)S(1)} all-gather(f32[1,1,128]{2,1,0:T(1,128)S(1)} %slice_bitcast_fusion), channel_id=4, replica_groups=mesh['parts'=2,'warp'=4,'weft'=2,'ply'=2] {'warp','weft','ply'}, dimensions={0}, use_global_device_ids=true | all-gather | bytes 8704 | tf_op jit(solution)/shard_map/all_gather | solution.py:137
  532.9 31.4 %all-reduce.2 = f32[128]{0:T(128)S(1)} all-reduce(f32[128]{0:T(128)S(1)} %dynamic-update-slice.2), channel_id=1, replica_groups=mesh['parts'=2,'warp'=4,'weft'=2,'ply'=2] {'warp','weft','ply'}, use_global_device_ids=true, to_apply=%add.2 | all-reduce | flops 128 | bytes 1024
  564.2 12.6 %gather_fusion.14 = f32[2048]{0:T(1024)S(1)} fusion(f32[128]{0:T(128)S(1)} %all-reduce.2, s32[2048]{0:T(1024)S(1)} %broadcast_clamp_fusion), kind=kCustom, calls=%fused_computation.14 | custom fusion | bytes 24576 | tf_op jit(solution)/shard_map/gather | solution.py:144
  579.2 8.8 %ragged-dot-none = f32[512,512]{1,0:T(8,128)} custom-call(s32[1]{0:T(128)} %get-tuple-element.27, s32[4]{0:T(128)} %get-tuple-element.28, s32[4]{0:T(128)} %get-tuple-element.29, s32[4]{0:T(128)} %get-tuple-element.30, s32[1]{0:T(128)} %get-tuple-element.27, f32[512,512]{1,0:T(8,128)} %gather_fusion.12, f32[3,512,512]{2,1,0:T(8,128)} %param.16), custom_call_target="tpu_custom_call" | custom-call | flops 268435456 | bytes 5242892 | tf_op jit(solution)/shard_map/ragged_dot_general/ragged-dot-none
  608.1 30.7 %psum.47 = f32[]{:T(128)} all-reduce(f32[]{:T(128)} %fusion.21), channel_id=1, replica_groups=mesh['parts'=2,'warp'=4,'weft'=2,'ply'=2] {'warp','weft','ply'}, use_global_device_ids=true, to_apply=%region_23.24 | all-reduce | flops 1 | bytes 8 | tf_op jit(solution)/shard_map/psum | solution.py:149
  (283 shorter events, 164.8 us)
Async XLA Ops:
  29.4 6.2 collective-permute-start
  32.6 5.1 collective-permute-start.1
  38.5 7.7 %collective-permute-start.2 = (f32[6,1,256]{2,1,0:T(1,128)S(1)}, f32[6,1,256]{2,1,0:T(1,128)S(1)}, u32[]{:S(2)}, u32[]{:S(2)}) collective-permute-start(f32[6,1,256]{2,1,0:T(1,128)S(1)} %get-tuple-element.103), channel_id=1, source_target_pairs={{0,2},{1,3},{4,6},{5,7},{8,10},{9,11},{12,14},{13,15},{16,18},{17,... | collective-permute-start | bytes 18440 | tf_op jit(solution)/shard_map/ppermute | solution.py:17
  41.9 5.5 collective-permute-start.3
  180.7 2.7 collective-permute-start.4
  182.0 3.2 collective-permute-start.5
  185.3 2.8 collective-permute-start.6
  186.5 5.5 collective-permute-start.7
  244.1 3.7 collective-permute-start.8
  245.4 3.2 collective-permute-start.9
  248.7 2.7 collective-permute-start.10
  250.0 5.5 collective-permute-start.11
  386.9 2.7 collective-permute-start.12
  388.2 3.2 collective-permute-start.13
  391.4 2.7 collective-permute-start.14
  392.7 5.5 collective-permute-start.15
  451.2 3.9 collective-permute-start.16
  452.7 3.2 collective-permute-start.17
  456.0 3.7 collective-permute-start.18
  457.3 5.5 collective-permute-start.19
  594.4 2.8 collective-permute-start.20
  595.8 3.2 collective-permute-start.21
  599.1 2.7 collective-permute-start.22
  600.4 5.5 collective-permute-start.23
  (45 other events, 1776.6 us)
